TPU v7x, 256 devices: a whole 4x4x8 slice. The times are simulated.
256 devices in a mesh: band: 64 (over y, z, core), rep: 4 (over x).
Axes of the slice: x: 4, y: 4, z: 8, core: 2. Of those that a mesh axis runs over, the one named last changes fastest.
Arguments:
- embeddings: bfloat16 [128, 32768], P('rep', 'band'), may hold values from -6 to 6
- route: int32 [32768, 1], P('band'), may hold values from 0 to 63; in each aligned block of 512 rows (0 to 511, 512 to 1023, ...) at most 20 rows name the same one
- place: bfloat16 [2, 32768], P(None, 'band'), may hold values from 0 to 1
- scales: float32 [4], replicated, may hold values from 0.25 to 1
- first_weight: bfloat16 [512, 512], replicated, may hold values from -0.25 to 0.25
- first_bias: float32 [512], replicated, may hold values from -3 to 3
- second_weight: bfloat16 [512, 512], replicated, may hold values from -0.25 to 0.25
- out_cotangent: bfloat16 [512, 768, 256], P(None, ('band', 'rep')), may hold values from -6 to 6
Outputs:
- embed_gradient: float32 [128, 32768], P('rep', 'band')
- first_weight_gradient: float32 [512, 512], replicated
- first_bias_gradient: float32 [512], replicated
- second_weight_gradient: float32 [512, 512], replicated
Inputs may be any that keep to these rules, and one draw needn't show every extreme that they name: `route`: within the 512 reports of one feed (aligned blocks of rows), at most 20 name the same band, and in some block exactly 20 do.
All inputs are finite; a program needn't handle non-finite values.
Results may differ from a plain program's by a relative error of at most 0.0063.
Values may be sent and summed in bfloat16 or wider, within the bound.
A program may use at most 128 MiB of HBM per device.

v0:
```python
import jax
import jax.numpy as jnp
from jax import lax
from jax.sharding import PartitionSpec as P

root_two_pi = 0.7978845608028654
cubic = 0.044715


def gelu_value(value):
    inner = root_two_pi * (value + cubic * value * value * value)
    return 0.5 * value * (1.0 + jnp.tanh(inner))


def gelu_slope(value):
    tangent = jnp.tanh(root_two_pi * (value + cubic * value * value * value))
    return 0.5 * (1.0 + tangent) + 0.5 * value * (1.0 - tangent * tangent) * root_two_pi * (
        1.0 + 3.0 * cubic * value * value
    )


def kernel_factors(geometry, block, scales, lat_rows, columns):
    north_fraction = geometry[0]
    east_fraction = geometry[1]
    valid = geometry[2]
    centre_rows = jnp.arange(lat_rows, dtype=jnp.float32) + 0.5
    north_gap = (
        ((1 - block).astype(jnp.float32) * lat_rows)[None, :]
        + centre_rows[:, None]
        - (north_fraction * lat_rows)[None, :]
    )
    east_gap = (jnp.arange(columns, dtype=jnp.float32) + 0.5)[:, None] - (east_fraction * columns)[
        None, :
    ]
    reach = scales * lat_rows
    inverse = 0.5 / (reach * reach)
    row_kernel = (
        jnp.exp(-(north_gap * north_gap)[None] * inverse[:, None, None]) * valid[None, None, :]
    ).astype(jnp.bfloat16)
    column_kernel = jnp.exp(-(east_gap * east_gap)[None] * inverse[:, None, None]).astype(
        jnp.bfloat16
    )
    return (row_kernel, column_kernel)


def splat(embedded, row_kernel, column_kernel):
    channels = embedded.shape[0]
    levels, lat_rows, slots = row_kernel.shape
    columns = column_kernel.shape[1]
    sums = []
    weights = []
    for level in range(levels):
        weighted = (embedded[:, None, :] * row_kernel[level][None]).reshape(
            channels * lat_rows, slots
        )
        sums.append(
            lax.dot_general(
                weighted,
                column_kernel[level],
                (((1,), (1,)), ((), ())),
                preferred_element_type=jnp.float32,
            )
        )
        weights.append(
            lax.dot_general(
                row_kernel[level],
                column_kernel[level],
                (((1,), (1,)), ((), ())),
                preferred_element_type=jnp.float32,
            )
        )
    splatted = jnp.stack(sums).reshape(levels, channels, lat_rows * columns)
    density = jnp.stack(weights).reshape(levels, lat_rows * columns)
    features = (
        (splatted / (density[:, None, :] + 1.0))
        .transpose(1, 0, 2)
        .reshape(channels * levels, lat_rows * columns)
        .astype(jnp.bfloat16)
    )
    return (features, density)


def spread_back(gradient, row_kernel, column_kernel):
    levels, lat_rows, slots = row_kernel.shape
    columns = column_kernel.shape[1]
    channels = gradient.shape[0] // levels
    grid = gradient.reshape(channels, levels, lat_rows * columns)
    total = jnp.zeros((channels, slots), jnp.float32)
    for level in range(levels):
        slab = grid[:, level].reshape(channels * lat_rows, columns)
        along = jnp.dot(slab, column_kernel[level], preferred_element_type=jnp.float32).reshape(
            channels, lat_rows, slots
        )
        total = total + jnp.sum(along * row_kernel[level][None].astype(jnp.float32), axis=1)
    return total


def band_ranks(route_rows, bands):
    owner = route_rows[:, 0]
    onehot = (owner[:, None] == jnp.arange(bands, dtype=jnp.int32)[None, :]).astype(jnp.int32)
    running = jnp.cumsum(onehot, axis=0)
    return (owner, jnp.sum((running - 1) * onehot, axis=1))


def on_device(
    embeddings, route, place, scales, first_weight, first_bias, second_weight, out_cotangent
):
    channels, reports = embeddings.shape
    bands = lax.axis_size("band")
    parts = lax.axis_size("rep")
    quarter = lax.axis_index("rep")
    capacity = max(2, 5 * reports // (2 * bands))
    sub_rows = out_cotangent.shape[1]
    lat_rows = sub_rows * parts
    columns = out_cotangent.shape[2]
    levels = scales.shape[0]
    owner, rank = band_ranks(route, bands)
    packed = jnp.concatenate([embeddings, place, jnp.ones((1, reports), jnp.bfloat16)], axis=0)
    rows = channels + 3
    span = 3 * capacity
    outgoing = jnp.zeros((rows, bands * span), jnp.bfloat16)
    for offset in range(3):
        target = owner + 1 - offset
        inside = (target >= 0) & (target < bands)
        where_to = jnp.where(inside, target * span + offset * capacity + rank, bands * span)
        outgoing = outgoing.at[:, where_to].set(packed, mode="drop")
    nearby = lax.all_to_all(outgoing, "band", split_axis=1, concat_axis=1, tiled=True)
    block = jnp.arange(bands * span, dtype=jnp.int32) // capacity % 3
    geometry = nearby[channels:].astype(jnp.float32)
    row_kernel, column_kernel = kernel_factors(geometry, block, scales, lat_rows, columns)
    features, density = splat(nearby[:channels], row_kernel, column_kernel)
    cotangent = out_cotangent.reshape(out_cotangent.shape[0], sub_rows * columns)
    mine = lax.all_to_all(features, "rep", split_axis=1, concat_axis=0, tiled=True)
    local_density = lax.dynamic_slice_in_dim(
        density.reshape(levels, lat_rows, columns), quarter * sub_rows, sub_rows, 1
    ).reshape(levels, sub_rows * columns)
    preact = (
        lax.dot_general(
            first_weight, mine, (((0,), (0,)), ((), ())), preferred_element_type=jnp.float32
        )
        + first_bias[:, None]
    )
    hidden = gelu_value(preact).astype(jnp.bfloat16)
    pre_gradient = (
        jnp.dot(second_weight, cotangent, preferred_element_type=jnp.float32) * gelu_slope(preact)
    ).astype(jnp.bfloat16)
    first_sum = lax.dot_general(
        mine, pre_gradient, (((1,), (1,)), ((), ())), preferred_element_type=jnp.float32
    )
    second_sum = lax.dot_general(
        hidden, cotangent, (((1,), (1,)), ((), ())), preferred_element_type=jnp.float32
    )
    bias_sum = jnp.sum(pre_gradient.astype(jnp.float32), axis=1)
    feature_gradient = jnp.dot(first_weight, pre_gradient, preferred_element_type=jnp.float32)
    count = sub_rows * columns
    cell_part = (
        (feature_gradient.reshape(-1, levels, count) / (local_density[None] + 1.0))
        .reshape(-1, count)
        .astype(jnp.bfloat16)
    )
    splat_gradient = lax.all_to_all(cell_part, "rep", split_axis=0, concat_axis=1, tiled=True)
    totals = lax.psum((first_sum, second_sum, bias_sum), ("band", "rep"))
    slot_gradient = spread_back(splat_gradient, row_kernel, column_kernel)
    backward = lax.all_to_all(slot_gradient, "band", split_axis=1, concat_axis=1, tiled=True)
    embed_gradient = jnp.zeros((channels, reports), jnp.float32)
    for offset in range(3):
        target = owner + 1 - offset
        inside = (target >= 0) & (target < bands)
        where_from = jnp.where(inside, target * span + offset * capacity + rank, 0)
        embed_gradient = embed_gradient + jnp.where(inside[None, :], backward[:, where_from], 0.0)
    return (embed_gradient, totals[0], totals[2], totals[1])


def solution(mesh):
    return jax.shard_map(
        on_device,
        mesh=mesh,
        in_specs=(
            P("rep", "band"),
            P("band", None),
            P(None, "band"),
            P(),
            P(),
            P(),
            P(),
            P(None, ("band", "rep"), None),
        ),
        out_specs=(P("rep", "band"), P(), P(), P()),
        check_vma=False,
    )
```

profile of v0, /device:TPU:2, one launch (start us, length us, event | category | flops | bytes accessed | tf_op | source)
XLA Modules:
  0.0 443.6 jit_solution(7938262040771985791)
XLA Ops:
  7.2 0.8 fusion.67
  7.9 1.2 reduce-window.6
  9.4 0.8 fusion.66
  10.2 0.7 compare_select_fusion.2
  11.0 0.9 maximum_bitcast_fusion
  12.0 2.1 scatter_custom_fusion
  14.1 2.3 scatter_fusion
  16.5 2.3 scatter_fusion.1
  19.1 0.7 copy.45
  19.8 1.9 reshape.419
  21.7 12.3 %all-to-all-start = ((bf16[64,2,1050]{2,1,0:T(2,128)(2,1)}), bf16[64,2,1050]{2,1,0:T(2,128)(2,1)S(1)}, u32[]{:S(2)}, u32[]{:S(2)}) async-start(bf16[64,2,1050]{2,1,0:T(2,128)(2,1)} %reshape.419), calls=%async_computation | async-start | bytes 589824 | tf_op jit(solution)/shard_map/all_to_all | solution.py:127
  34.1 12.5 %all-to-all-done = bf16[64,2,1050]{2,1,0:T(2,128)(2,1)S(1)} async-done(((bf16[64,2,1050]{2,1,0:T(2,128)(2,1)}), bf16[64,2,1050]{2,1,0:T(2,128)(2,1)S(1)}, u32[]{:S(2)}, u32[]{:S(2)}) %all-to-all-start) | async-done | bytes 268832 | tf_op jit(solution)/shard_map/all_to_all | solution.py:127
  46.6 0.8 reshape.420
  48.3 0.8 copy-done.2
  49.1 1.1 fusion.87
  50.7 2.9 exponential_convert_fusion
  53.7 1.7 fusion.4
  55.3 0.7 fusion.8
  56.0 0.7 fusion.12
  57.6 0.8 mul.298
  58.4 6.8 %broadcast_multiply_fusion.3 = (bf16[32,12,3840]{2,1,0:T(8,128)(2,1)}, bf16[32,12,3840]{2,1,0:T(8,128)(2,1)}, bf16[32,12,3840]{2,1,0:T(8,128)(2,1)}, bf16[32,12,3840]{2,1,0:T(8,128)(2,1)}) fusion(bf16[12,3840]{1,0:T(8,128)(2,1)} %get-tuple-element.32, bf16[32,3840]{1,0:T(8,128)(2,1)S(1)} %mul.298, bf16[12,3840]{1,0:T(8,128)(2,1)} %get-tuple-element.31, ...), kind=kLoop, calls=%fused_computation.37 | loop fusion | flops 5898240 | bytes 12410880 | tf_op jit(solution)/shard_map/mul | solution.py:53
  65.2 3.9 mul.315
  69.1 3.2 fusion.18
  72.3 2.1 stack.55
  74.5 3.9 mul.326
  78.4 3.3 fusion.14
  81.6 2.2 stack.56
  83.8 3.9 mul.330
  87.7 3.2 fusion.10
  90.9 2.1 stack.57
  93.1 4.1 mul.334
  97.2 3.2 fusion.6
  100.4 1.4 stack.58
  102.0 2.8 fusion.54
  105.0 1.0 copy.51
  106.0 4.8 %all-to-all-start.1 = ((bf16[128,4,768]{2,0,1:T(8,128)(2,1)}), bf16[128,4,768]{2,0,1:T(8,128)(2,1)S(1)}, u32[]{:S(2)}, u32[]{:S(2)}) async-start(bf16[128,4,768]{2,0,1:T(8,128)(2,1)} %copy.51), calls=%async_computation.1 | async-start | bytes 1572864 | tf_op jit(solution)/shard_map/all_to_all | solution.py:133
  110.8 1.2 copy.39
  112.2 1.8 div.37
  114.0 7.9 %all-to-all-done.1 = bf16[128,4,768]{2,0,1:T(8,128)(2,1)S(1)} async-done(((bf16[128,4,768]{2,0,1:T(8,128)(2,1)}), bf16[128,4,768]{2,0,1:T(8,128)(2,1)S(1)}, u32[]{:S(2)}, u32[]{:S(2)}) %all-to-all-start.1) | async-done | bytes 786464 | tf_op jit(solution)/shard_map/all_to_all | solution.py:133
  121.9 0.6 convolution_add_fusion
  122.6 1.3 convert_reduce_fusion
  124.6 1.5 fusion.39
  126.0 5.3 %all-to-all-start.2 = ((bf16[4,128,768]{2,1,0:T(8,128)(2,1)}), bf16[4,128,768]{2,1,0:T(8,128)(2,1)S(1)}, u32[]{:S(2)}, u32[]{:S(2)}) async-start(bf16[4,128,768]{2,1,0:T(8,128)(2,1)} %bitcast.182), calls=%async_computation.2 | async-start | bytes 1572864 | tf_op jit(solution)/shard_map/all_to_all | solution.py:161
  131.4 3.0 fusion.53
  134.4 6.8 %all-to-all-done.2 = bf16[4,128,768]{2,1,0:T(8,128)(2,1)S(1)} async-done(((bf16[4,128,768]{2,1,0:T(8,128)(2,1)}), bf16[4,128,768]{2,1,0:T(8,128)(2,1)S(1)}, u32[]{:S(2)}, u32[]{:S(2)}) %all-to-all-start.2) | async-done | bytes 786464 | tf_op jit(solution)/shard_map/all_to_all | solution.py:161
  142.1 3.4 slice_reduce_fusion.2
  145.6 2.7 fusion.23
  148.3 2.6 fusion.20
  150.9 1.0 fusion.26
  151.9 1.0 fusion.29
  153.0 1.5 add.265
  155.2 2.6 reshape.421
  157.8 5.9 %all-to-all-start.3 = ((f32[64,1,1920]{2,1,0:T(1,128)}), f32[64,1,1920]{2,1,0:T(1,128)S(1)}, u32[]{:S(2)}, u32[]{:S(2)}) async-start(f32[64,1,1920]{2,1,0:T(1,128)} %reshape.421), calls=%async_computation.3 | async-start | bytes 983040 | tf_op jit(solution)/shard_map/all_to_all | solution.py:164
  163.8 2.7 fusion.90
  166.6 77.1 %psum.22 = f32[512]{0:T(512)} all-reduce(f32[512]{0:T(512)S(1)} %get-tuple-element.46), channel_id=1, replica_groups=mesh['band'=64,'rep'=4] {'band','rep'}, use_global_device_ids=true, to_apply=%region_12.13 | all-reduce | flops 512 | bytes 4096 | tf_op jit(solution)/shard_map/psum | solution.py:162
  244.2 1.8 reduce.22
  246.0 1.5 reshape.422
  249.3 1.0 gather_fusion
  250.4 1.0 gather_fusion.1
  251.4 1.0 gather_fusion.2
  252.8 0.7 copy.63
  253.5 179.7 %all-reduce.3.cloned.1.call-done = (f32[512,512]{1,0:T(8,128)}, f32[512,512]{1,0:T(8,128)}) async-done(((f32[512,512]{1,0:T(8,128)}, f32[512,512]{1,0:T(8,128)}), (f32[512,512]{1,0:T(8,128)}, f32[512,512]{1,0:T(8,128)})) %all-reduce.3.cloned.1.call-update) | async-done | bytes 2097168 | tf_op jit(solution)/shard_map/psum | solution.py:162
  433.2 2.4 copy.100
  435.6 1.0 copy.101
  (84 shorter events, 8.8 us)
Async XLA Ops:
  7.2 114.8 %copy-start = (bf16[512,512]{1,0:T(8,128)(2,1)S(1)}, bf16[512,512]{1,0:T(8,128)(2,1)}, u32[]{:S(2)}) copy-start(bf16[512,512]{1,0:T(8,128)(2,1)} %param.12) | copy-start | bytes 1572868
  19.1 15.0 %copy-start.15 = (f32[4]{0:T(128)S(1)}, f32[4]{0:T(128)}, u32[]{:S(2)}) copy-start(f32[4]{0:T(128)} %param.11) | copy-start | bytes 52
  21.7 24.9 %all-to-all-start = ((bf16[64,2,1050]{2,1,0:T(2,128)(2,1)}), bf16[64,2,1050]{2,1,0:T(2,128)(2,1)S(1)}, u32[]{:S(2)}, u32[]{:S(2)}) async-start(bf16[64,2,1050]{2,1,0:T(2,128)(2,1)} %reshape.419), calls=%async_computation | async-start | bytes 589824 | tf_op jit(solution)/shard_map/all_to_all | solution.py:127
  48.3 0.8 copy-start.2
  53.6 3.1 copy-start.1
  53.7 1.7 copy-start.3
  105.0 5.8 %copy-start.6 = (bf16[512,3,256]{2,0,1:T(8,128)(2,1)S(1)}, bf16[512,3,256]{2,0,1:T(8,128)(2,1)}, u32[]{:S(2)}) copy-start(bf16[512,3,256]{2,0,1:T(8,128)(2,1)} %param.15) | copy-start | bytes 2359300
  106.0 15.9 %all-to-all-start.1 = ((bf16[128,4,768]{2,0,1:T(8,128)(2,1)}), bf16[128,4,768]{2,0,1:T(8,128)(2,1)S(1)}, u32[]{:S(2)}, u32[]{:S(2)}) async-start(bf16[128,4,768]{2,0,1:T(8,128)(2,1)} %copy.51), calls=%async_computation.1 | async-start | bytes 1572864 | tf_op jit(solution)/shard_map/all_to_all | solution.py:133
  112.2 9.7 %copy-start.14 = (f32[512]{0:T(512)S(1)}, f32[512]{0:T(512)}, u32[]{:S(2)}) copy-start(f32[512]{0:T(512)} %param.13) | copy-start | bytes 6148
  114.0 8.6 %copy-start.7 = (bf16[512,3,256]{0,2,1:T(8,128)(2,1)S(1)}, bf16[512,3,256]{0,2,1:T(8,128)(2,1)}, u32[]{:S(2)}) copy-start(bf16[512,3,256]{0,2,1:T(8,128)(2,1)} %copy.39) | copy-start | bytes 2359300
  114.0 8.6 %copy-start.13 = (bf16[512,512]{1,0:T(8,128)(2,1)S(1)}, bf16[512,512]{1,0:T(8,128)(2,1)}, u32[]{:S(2)}) copy-start(bf16[512,512]{1,0:T(8,128)(2,1)} %param.14) | copy-start | bytes 1572868
  122.6 1.4 copy-start.16
  122.6 2.0 copy-start.4
  123.9 2.1 copy-start.8
  126.0 15.2 %all-to-all-start.2 = ((bf16[4,128,768]{2,1,0:T(8,128)(2,1)}), bf16[4,128,768]{2,1,0:T(8,128)(2,1)S(1)}, u32[]{:S(2)}, u32[]{:S(2)}) async-start(bf16[4,128,768]{2,1,0:T(8,128)(2,1)} %bitcast.182), calls=%async_computation.2 | async-start | bytes 1572864 | tf_op jit(solution)/shard_map/all_to_all | solution.py:161
  142.1 8.7 %slice-start = ((s8[7864320]{0:T(1024)(128)(4,1)}), s8[3670016]{0:T(1024)(128)(4,1)S(1)}, s32[]{:S(2)}) async-start(s8[7864320]{0:T(1024)(128)(4,1)} %bitcast.170), calls=%async_computation.5 | async-start | bytes 7340032
  145.5 2.7 copy-start.11
  145.5 5.3 %slice-start.1 = ((s8[7864320]{0:T(1024)(128)(4,1)}), s8[4194304]{0:T(1024)(128)(4,1)S(1)}, s32[]{:S(2)}) async-start(s8[7864320]{0:T(1024)(128)(4,1)} %bitcast.170), calls=%async_computation.6 | async-start | bytes 8388608
  148.2 2.6 copy-start.10
  150.9 1.0 copy-start.9
  157.8 85.9 %all-to-all-start.3 = ((f32[64,1,1920]{2,1,0:T(1,128)}), f32[64,1,1920]{2,1,0:T(1,128)S(1)}, u32[]{:S(2)}, u32[]{:S(2)}) async-start(f32[64,1,1920]{2,1,0:T(1,128)} %reshape.421), calls=%async_computation.3 | async-start | bytes 983040 | tf_op jit(solution)/shard_map/all_to_all | solution.py:164
  163.7 2.8 copy-start.12
  163.7 269.5 %all-reduce.3.cloned.1.call-start = ((), (), s32[]{:S(2)}) async-start(), calls=%async_computation.4 | async-start | bytes 4194304 | tf_op jit(solution)/shard_map/psum | solution.py:162
  433.2 2.4 copy-start.5
Sparse Core Ops, SparseCore 0:
  170.7 262.4 all-reduce.2
where the time goes:
time: 451 us; the launch traced here: 444 us
  waiting for transfers between devices  207 us (46%)
  blocking collectives  77.1 us (17%)
  local copies, waits for them, and re-layouts  61.9 us (14%)
  matrix products  32.9 us (7%)
  starting transfers between devices  28.4 us (6%)
  other arithmetic  21.3 us (5%)
  between operations  14.9 us (3%)
    psum x1, waiting for transfers between devices, on_device(): totals = lax.psum((first_sum, second_sum, bias_sum), ('band', 'rep'))  180 us
    psum x1, blocking collectives, on_device(): totals = lax.psum((first_sum, second_sum, bias_sum), ('band', 'rep'))  77.1 us
    mul x5, local copies, waits for them, and re-layouts, splat(): embedded[:, None, :] * row_kernel[level][None]  16.6 us
    unnamed x51, local copies, waits for them, and re-layouts  13.7 us
    dot_general x4, matrix products, splat(): lax.dot_general(weighted, column_kernel[level], (((1,), (1,)), ((), ())),...  13 us
    all_to_all x1, waiting for transfers between devices, on_device(): lax.all_to_all(outgoing, 'band', split_axis=1, concat_axis=1, tiled=True)  12.5 us
    all_to_all x1, starting transfers between devices, on_device(): lax.all_to_all(outgoing, 'band', split_axis=1, concat_axis=1, tiled=True)  12.3 us
  transfers between devices with their start and end apart: 5, of which 4 were waited for; matrix products, arithmetic and copies ran while one was open for 4% of the time, Pallas kernels for 0%

commit v1 on v0

--- a/solution.py
+++ b/solution.py
@@ -159,7 +159,9 @@
         .astype(jnp.bfloat16)
     )
     splat_gradient = lax.all_to_all(cell_part, "rep", split_axis=0, concat_axis=1, tiled=True)
-    totals = lax.psum((first_sum, second_sum, bias_sum), ("band", "rep"))
+    totals = (first_sum, second_sum, bias_sum)
+    for name in ("rep", "band"):
+        totals = lax.psum(totals, name)
     slot_gradient = spread_back(splat_gradient, row_kernel, column_kernel)
     backward = lax.all_to_all(slot_gradient, "band", split_axis=1, concat_axis=1, tiled=True)
     embed_gradient = jnp.zeros((channels, reports), jnp.float32)

time: 451 us -> 408 us (0.905)
  waiting for transfers between devices: 207 us -> 105 us
  blocking collectives: 77.1 us -> 137 us
    psum x1 -> x2, waiting for transfers between devices: 180 us -> 79.3 us  [on_device(): totals = lax.psum(totals, name)]
    psum x1 -> x2, blocking collectives: 77.1 us -> 137 us  [on_device(): totals = lax.psum(totals, name)]
    unnamed x51 -> x55, local copies, waits for them, and re-layouts: 13.7 us -> 13.7 us
  transfers between devices with their start and end apart: 5 -> 6, of which waited for: 4 -> 5; matrix products, arithmetic and copies ran while one was open for 4% -> 8% of each run, Pallas kernels for 0% -> 0%
where the time goes in v1:
time: 408 us; the launch traced here: 401 us
  blocking collectives  137 us (34%)
  waiting for transfers between devices  105 us (26%)
  local copies, waits for them, and re-layouts  61.9 us (15%)
  matrix products  31.7 us (8%)
  starting transfers between devices  28.7 us (7%)
  other arithmetic  21.3 us (5%)
  between operations  14.9 us (4%)
    psum x2, blocking collectives, on_device(): totals = lax.psum(totals, name)  137 us
    psum x2, waiting for transfers between devices, on_device(): totals = lax.psum(totals, name)  79.3 us
    mul x5, local copies, waits for them, and re-layouts, splat(): embedded[:, None, :] * row_kernel[level][None]  16.6 us
    unnamed x55, local copies, waits for them, and re-layouts  13.7 us
    dot_general x4, matrix products, splat(): lax.dot_general(weighted, column_kernel[level], (((1,), (1,)), ((), ())),...  13 us
    all_to_all x1, waiting for transfers between devices, on_device(): lax.all_to_all(outgoing, 'band', split_axis=1, concat_axis=1, tiled=True)  12.5 us
    all_to_all x1, starting transfers between devices, on_device(): lax.all_to_all(outgoing, 'band', split_axis=1, concat_axis=1, tiled=True)  12.3 us
  transfers between devices with their start and end apart: 6, of which 5 were waited for; matrix products, arithmetic and copies ran while one was open for 8% of the time, Pallas kernels for 0%

profile of v1, /device:TPU:2, one launch (start us, length us, event | category | flops | bytes accessed | tf_op | source)
XLA Modules:
  0.0 400.6 jit_solution(18087226297286206863)
XLA Ops:
  7.2 0.8 fusion.67
  7.9 1.2 reduce-window.6
  9.4 0.8 fusion.66
  10.2 0.7 compare_select_fusion.2
  11.0 0.9 maximum_bitcast_fusion
  12.0 2.1 scatter_custom_fusion
  14.1 2.3 scatter_fusion
  16.5 2.3 scatter_fusion.1
  19.1 0.7 copy.45
  19.8 1.9 reshape.419
  21.7 12.3 %all-to-all-start = ((bf16[64,2,1050]{2,1,0:T(2,128)(2,1)}), bf16[64,2,1050]{2,1,0:T(2,128)(2,1)S(1)}, u32[]{:S(2)}, u32[]{:S(2)}) async-start(bf16[64,2,1050]{2,1,0:T(2,128)(2,1)} %reshape.419), calls=%async_computation | async-start | bytes 589824 | tf_op jit(solution)/shard_map/all_to_all | solution.py:127
  34.1 12.5 %all-to-all-done = bf16[64,2,1050]{2,1,0:T(2,128)(2,1)S(1)} async-done(((bf16[64,2,1050]{2,1,0:T(2,128)(2,1)}), bf16[64,2,1050]{2,1,0:T(2,128)(2,1)S(1)}, u32[]{:S(2)}, u32[]{:S(2)}) %all-to-all-start) | async-done | bytes 268832 | tf_op jit(solution)/shard_map/all_to_all | solution.py:127
  46.6 0.8 reshape.420
  48.3 0.8 copy-done.2
  49.1 1.1 fusion.87
  50.7 2.9 exponential_convert_fusion
  53.7 1.7 fusion.4
  55.3 0.7 fusion.8
  57.6 0.8 mul.298
  58.4 6.8 %broadcast_multiply_fusion.3 = (bf16[32,12,3840]{2,1,0:T(8,128)(2,1)}, bf16[32,12,3840]{2,1,0:T(8,128)(2,1)}, bf16[32,12,3840]{2,1,0:T(8,128)(2,1)}, bf16[32,12,3840]{2,1,0:T(8,128)(2,1)}) fusion(bf16[12,3840]{1,0:T(8,128)(2,1)} %get-tuple-element.34, bf16[32,3840]{1,0:T(8,128)(2,1)S(1)} %mul.298, bf16[12,3840]{1,0:T(8,128)(2,1)} %get-tuple-element.33, ...), kind=kLoop, calls=%fused_computation.37 | loop fusion | flops 5898240 | bytes 12410880 | tf_op jit(solution)/shard_map/mul | solution.py:53
  65.2 3.9 mul.315
  69.1 3.2 fusion.18
  72.3 2.1 stack.55
  74.5 3.9 mul.326
  78.4 3.3 fusion.14
  81.6 2.2 stack.56
  83.8 3.9 mul.330
  87.7 3.2 fusion.10
  90.9 2.1 stack.57
  93.1 4.1 %mul.334 = bf16[384,3840]{1,0:T(8,128)(2,1)S(1)} reshape(bf16[32,12,3840]{2,1,0:T(8,128)(2,1)} %get-tuple-element.38) | data formatting | bytes 5898240 | tf_op jit(solution)/shard_map/mul | solution.py:53
  97.2 3.2 fusion.6
  100.4 1.4 stack.58
  102.0 2.8 fusion.54
  105.0 1.0 copy.51
  106.0 4.8 %all-to-all-start.1 = ((bf16[128,4,768]{2,0,1:T(8,128)(2,1)}), bf16[128,4,768]{2,0,1:T(8,128)(2,1)S(1)}, u32[]{:S(2)}, u32[]{:S(2)}) async-start(bf16[128,4,768]{2,0,1:T(8,128)(2,1)} %copy.51), calls=%async_computation.1 | async-start | bytes 1572864 | tf_op jit(solution)/shard_map/all_to_all | solution.py:133
  110.8 1.2 copy.39
  112.2 1.7 div.37
  114.0 8.0 %all-to-all-done.1 = bf16[128,4,768]{2,0,1:T(8,128)(2,1)S(1)} async-done(((bf16[128,4,768]{2,0,1:T(8,128)(2,1)}), bf16[128,4,768]{2,0,1:T(8,128)(2,1)S(1)}, u32[]{:S(2)}, u32[]{:S(2)}) %all-to-all-start.1) | async-done | bytes 786464 | tf_op jit(solution)/shard_map/all_to_all | solution.py:133
  122.6 1.3 convert_reduce_fusion
  124.6 1.5 fusion.39
  126.1 4.9 %all-to-all-start.2 = ((bf16[4,128,768]{2,1,0:T(8,128)(2,1)}), bf16[4,128,768]{2,1,0:T(8,128)(2,1)S(1)}, u32[]{:S(2)}, u32[]{:S(2)}) async-start(bf16[4,128,768]{2,1,0:T(8,128)(2,1)} %bitcast.182), calls=%async_computation.2 | async-start | bytes 1572864 | tf_op jit(solution)/shard_map/all_to_all | solution.py:161
  131.4 2.8 fusion.90
  134.2 1.6 fusion.53
  135.9 5.3 %all-to-all-done.2 = bf16[4,128,768]{2,1,0:T(8,128)(2,1)S(1)} async-done(((bf16[4,128,768]{2,1,0:T(8,128)(2,1)}), bf16[4,128,768]{2,1,0:T(8,128)(2,1)S(1)}, u32[]{:S(2)}, u32[]{:S(2)}) %all-to-all-start.2) | async-done | bytes 786464 | tf_op jit(solution)/shard_map/all_to_all | solution.py:161
  142.2 3.4 slice_reduce_fusion.2
  145.6 2.7 fusion.23
  148.3 2.6 fusion.20
  150.9 1.0 fusion.26
  151.9 1.0 fusion.29
  153.0 1.5 add.271
  155.2 2.6 reshape.421
  157.8 6.2 %all-to-all-start.3 = ((f32[64,1,1920]{2,1,0:T(1,128)}), f32[64,1,1920]{2,1,0:T(1,128)S(1)}, u32[]{:S(2)}, u32[]{:S(2)}) async-start(f32[64,1,1920]{2,1,0:T(1,128)} %reshape.421), calls=%async_computation.3 | async-start | bytes 983040 | tf_op jit(solution)/shard_map/all_to_all | solution.py:166
  164.1 31.5 %all-reduce.7.cloned.1.call-done = (f32[512,512]{1,0:T(8,128)}, f32[512,512]{1,0:T(8,128)}) async-done(((f32[512,512]{1,0:T(8,128)}, f32[512,512]{1,0:T(8,128)}), (f32[512,512]{1,0:T(8,128)}, f32[512,512]{1,0:T(8,128)})) %all-reduce.7.cloned.1.call-update) | async-done | bytes 2097168 | tf_op jit(solution)/shard_map/psum | solution.py:164
  195.7 9.5 %psum.44 = f32[512]{0:T(512)S(1)} all-reduce(f32[512]{0:T(512)S(1)} %get-tuple-element.48), channel_id=1, replica_groups=mesh['band'=64,'rep'=4] {'rep'}, use_global_device_ids=true, to_apply=%region_13.14 | all-reduce | flops 512 | bytes 4096 | tf_op jit(solution)/shard_map/psum | solution.py:164
  205.1 127.5 %psum.45 = f32[512]{0:T(512)} all-reduce(f32[512]{0:T(512)S(1)} %psum.44), channel_id=1, replica_groups=mesh['band'=64,'rep'=4] {'band'}, use_global_device_ids=true, to_apply=%region_14.15 | all-reduce | flops 512 | bytes 4096 | tf_op jit(solution)/shard_map/psum | solution.py:164
  333.2 1.8 reduce.22
  335.0 1.5 reshape.422
  338.3 1.0 gather_fusion
  339.4 1.0 gather_fusion.1
  340.4 1.0 gather_fusion.2
  341.7 0.7 copy.63
  342.5 47.8 %all-reduce.5.cloned.1.call-done = (f32[512,512]{1,0:T(8,128)}, f32[512,512]{1,0:T(8,128)}) async-done(((f32[512,512]{1,0:T(8,128)}, f32[512,512]{1,0:T(8,128)}), (f32[512,512]{1,0:T(8,128)}, f32[512,512]{1,0:T(8,128)})) %all-reduce.5.cloned.1.call-update) | async-done | bytes 2097168 | tf_op jit(solution)/shard_map/psum | solution.py:164
  390.2 2.4 copy.102
  392.6 1.0 copy.103
  (92 shorter events, 10.4 us)
Async XLA Ops:
  7.2 114.8 %copy-start = (bf16[512,512]{1,0:T(8,128)(2,1)S(1)}, bf16[512,512]{1,0:T(8,128)(2,1)}, u32[]{:S(2)}) copy-start(bf16[512,512]{1,0:T(8,128)(2,1)} %param.12) | copy-start | bytes 1572868
  19.1 15.0 %copy-start.16 = (f32[4]{0:T(128)S(1)}, f32[4]{0:T(128)}, u32[]{:S(2)}) copy-start(f32[4]{0:T(128)} %param.11) | copy-start | bytes 52
  21.7 24.9 %all-to-all-start = ((bf16[64,2,1050]{2,1,0:T(2,128)(2,1)}), bf16[64,2,1050]{2,1,0:T(2,128)(2,1)S(1)}, u32[]{:S(2)}, u32[]{:S(2)}) async-start(bf16[64,2,1050]{2,1,0:T(2,128)(2,1)} %reshape.419), calls=%async_computation | async-start | bytes 589824 | tf_op jit(solution)/shard_map/all_to_all | solution.py:127
  48.3 0.8 copy-start.2
  53.6 3.1 copy-start.1
  53.7 1.7 copy-start.3
  105.0 5.8 %copy-start.6 = (bf16[512,3,256]{2,0,1:T(8,128)(2,1)S(1)}, bf16[512,3,256]{2,0,1:T(8,128)(2,1)}, u32[]{:S(2)}) copy-start(bf16[512,3,256]{2,0,1:T(8,128)(2,1)} %param.15) | copy-start | bytes 2359300
  106.0 15.9 %all-to-all-start.1 = ((bf16[128,4,768]{2,0,1:T(8,128)(2,1)}), bf16[128,4,768]{2,0,1:T(8,128)(2,1)S(1)}, u32[]{:S(2)}, u32[]{:S(2)}) async-start(bf16[128,4,768]{2,0,1:T(8,128)(2,1)} %copy.51), calls=%async_computation.1 | async-start | bytes 1572864 | tf_op jit(solution)/shard_map/all_to_all | solution.py:133
  112.2 9.7 %copy-start.15 = (f32[512]{0:T(512)S(1)}, f32[512]{0:T(512)}, u32[]{:S(2)}) copy-start(f32[512]{0:T(512)} %param.13) | copy-start | bytes 6148
  114.0 8.6 %copy-start.7 = (bf16[512,3,256]{0,2,1:T(8,128)(2,1)S(1)}, bf16[512,3,256]{0,2,1:T(8,128)(2,1)}, u32[]{:S(2)}) copy-start(bf16[512,3,256]{0,2,1:T(8,128)(2,1)} %copy.39) | copy-start | bytes 2359300
  114.0 8.6 %copy-start.14 = (bf16[512,512]{1,0:T(8,128)(2,1)S(1)}, bf16[512,512]{1,0:T(8,128)(2,1)}, u32[]{:S(2)}) copy-start(bf16[512,512]{1,0:T(8,128)(2,1)} %param.14) | copy-start | bytes 1572868
  122.6 1.4 copy-start.17
  122.6 2.0 copy-start.4
  123.9 2.1 copy-start.8
  126.1 15.2 %all-to-all-start.2 = ((bf16[4,128,768]{2,1,0:T(8,128)(2,1)}), bf16[4,128,768]{2,1,0:T(8,128)(2,1)S(1)}, u32[]{:S(2)}, u32[]{:S(2)}) async-start(bf16[4,128,768]{2,1,0:T(8,128)(2,1)} %bitcast.182), calls=%async_computation.2 | async-start | bytes 1572864 | tf_op jit(solution)/shard_map/all_to_all | solution.py:161
  131.0 64.6 %all-reduce.7.cloned.1.call-start = ((), (), s32[]{:S(2)}) async-start(), calls=%async_computation.5 | async-start | bytes 4194304 | tf_op jit(solution)/shard_map/psum | solution.py:164
  131.4 2.8 copy-start.18
  141.8 3.7 copy-start.12
  142.1 8.8 %slice-start = ((s8[7864320]{0:T(1024)(128)(4,1)}), s8[3670016]{0:T(1024)(128)(4,1)S(1)}, s32[]{:S(2)}) async-start(s8[7864320]{0:T(1024)(128)(4,1)} %bitcast.170), calls=%async_computation.6 | async-start | bytes 7340032
  145.6 2.7 copy-start.11
  145.6 5.3 %slice-start.1 = ((s8[7864320]{0:T(1024)(128)(4,1)}), s8[4194304]{0:T(1024)(128)(4,1)S(1)}, s32[]{:S(2)}) async-start(s8[7864320]{0:T(1024)(128)(4,1)} %bitcast.170), calls=%async_computation.7 | async-start | bytes 8388608
  148.3 2.6 copy-start.10
  150.9 1.0 copy-start.9
  155.2 40.5 %copy-start.13 = (s32[512,1]{0,1:T(1,128)S(1)}, s32[512,1]{0,1:T(1,128)}, u32[]{:S(2)}) copy-start(s32[512,1]{0,1:T(1,128)} %param.9) | copy-start | bytes 6148
  157.8 174.8 %all-to-all-start.3 = ((f32[64,1,1920]{2,1,0:T(1,128)}), f32[64,1,1920]{2,1,0:T(1,128)S(1)}, u32[]{:S(2)}, u32[]{:S(2)}) async-start(f32[64,1,1920]{2,1,0:T(1,128)} %reshape.421), calls=%async_computation.3 | async-start | bytes 983040 | tf_op jit(solution)/shard_map/all_to_all | solution.py:166
  164.0 226.2 %all-reduce.5.cloned.1.call-start = ((), (), s32[]{:S(2)}) async-start(), calls=%async_computation.4 | async-start | bytes 4194304 | tf_op jit(solution)/shard_map/psum | solution.py:164
  390.2 2.4 copy-start.5
Sparse Core Ops, SparseCore 0:
  136.0 59.5 all-reduce.6
  199.5 190.6 all-reduce.4
